TPU v7x, 256 devices: a whole 4x4x8 slice. The times are simulated.
256 devices in a mesh: rows: 64 (over x, z, core), help: 4 (over y).
Axes of the slice: x: 4, y: 4, z: 8, core: 2. Of those that a mesh axis runs over, the one named last changes fastest.
Arguments:
- embeddings: bfloat16 [65536, 1024], P('rows'), may hold values from -192 to 192
- clusters: int32 [65536, 1], P('rows'), may hold values from 0 to 63; in each aligned block of 1024 rows (0 to 1023, 1024 to 2047, ...) at most 32 rows name the same one
Outputs:
- max_similarity: float32 [65536], P('rows')
Inputs may be any that keep to these rules, and one draw needn't show every extreme that they name: `clusters`: among the 1024 rows of one index of rows no cluster appears more than 32 times, and some cluster appears exactly 32 times there; every cluster appears somewhere.
All inputs are finite; a program needn't handle non-finite values.
Results may differ from a plain program's by a relative error of at most 0.00048.
Values may be sent and summed in bfloat16 or wider, within the bound.
A program may use at most 64 MiB of HBM per device.

v0:
```python
import jax
import jax.numpy as jnp
from jax import lax
from jax.sharding import PartitionSpec as P

EPSILON = 1e-06


def unit_rows(embeddings):
    values = embeddings.astype(jnp.float32)
    scale_inv = lax.rsqrt(jnp.sum(values * values, axis=1, keepdims=True) + EPSILON)
    return (values * scale_inv).astype(jnp.bfloat16)


def masked_rows(scores, allowed):
    return jnp.max(jnp.where(allowed, scores, -1.0), axis=1)


def pair_scores(left_rows, right_rows):
    return jnp.einsum("qd,kd->qk", left_rows, right_rows, preferred_element_type=jnp.float32)


def local(embeddings, clusters):
    row_count = embeddings.shape[0]
    owners = lax.axis_size("rows")
    helpers = lax.axis_size("help")
    most_rows = 2 * row_count // owners
    normed = unit_rows(embeddings)
    cluster_ids = clusters[:, 0]
    onehot = (cluster_ids[:, None] == jnp.arange(owners, dtype=jnp.int32)[None, :]).astype(
        jnp.float32
    )
    positions = jnp.arange(row_count, dtype=jnp.int32)
    earlier = (positions[None, :] < positions[:, None]).astype(jnp.float32)
    before = jnp.dot(
        earlier, onehot, precision=lax.Precision.HIGHEST, preferred_element_type=jnp.float32
    )
    row_rank = jnp.sum(before * onehot, axis=1).astype(jnp.int32)
    slot_index = cluster_ids * most_rows + row_rank
    global_ids = lax.axis_index("rows") * row_count + positions
    send_rows = (
        jnp.zeros((owners * most_rows, embeddings.shape[1]), jnp.bfloat16)
        .at[slot_index]
        .set(normed)
    )
    send_rows = send_rows.reshape(owners, most_rows, embeddings.shape[1])
    send_ids = jnp.full((owners * most_rows,), -1, jnp.int32).at[slot_index].set(global_ids)
    send_ids = send_ids.reshape(owners, most_rows)
    key_rows, key_ids = (
        lax.all_to_all(send_rows, "rows", split_axis=0, concat_axis=0, tiled=True),
        lax.all_to_all(send_ids, "rows", split_axis=0, concat_axis=0, tiled=True),
    )
    key_rows = key_rows.reshape(owners * most_rows, embeddings.shape[1])
    key_ids = key_ids.reshape(owners * most_rows)
    share_rows = owners * most_rows // helpers
    helper = lax.axis_index("help")
    mine_rows = lax.dynamic_slice_in_dim(key_rows, helper * share_rows, share_rows, 0)
    mine_ids = lax.dynamic_slice_in_dim(key_ids, helper * share_rows, share_rows, 0)
    scores = pair_scores(mine_rows, key_rows)
    allowed = (key_ids[None, :] >= 0) & (key_ids[None, :] < mine_ids[:, None])
    best_rows = masked_rows(scores, allowed)
    everything = lax.all_gather(best_rows, "help", axis=0, tiled=True)
    returned = lax.all_to_all(
        everything.reshape(owners, most_rows), "rows", split_axis=0, concat_axis=0, tiled=True
    )
    return returned.reshape(owners * most_rows)[slot_index]


def solution(mesh):
    placed = (P("rows", None), P("rows", None))
    return jax.shard_map(local, mesh=mesh, in_specs=placed, out_specs=P("rows"), check_vma=False)
```

profile of v0, /device:TPU:1, one launch (start us, length us, event | category | flops | bytes accessed | tf_op | source)
XLA Modules:
  0.0 180.7 jit_solution(11063315052054332383)
XLA Ops:
  0.0 0.0 copy-start
  0.0 1.4 fusion.8
  1.5 0.7 compare_select_fusion
  2.2 4.3 %scatter_custom_fusion = s32[2048]{0:T(1024)S(1)} fusion(s32[1024]{0:T(1024)S(1)} %bitcast.10, s32[1024]{0:T(1024)S(1)} %iota_add_fusion, s32[]{:T(128)} %constant.14.clone.1), kind=kCustom, calls=%fused_computation.22 | custom fusion | bytes 8196 | tf_op jit(solution)/shard_map/scatter | solution.py:47
  6.5 0.7 all_to_all.15
  7.2 13.0 %all-to-all-start = ((s32[64,1,32]{2,1,0:T(1,128)}), s32[64,1,32]{2,1,0:T(1,128)S(1)}, u32[]{:S(2)}, u32[]{:S(2)}) async-start(s32[64,1,32]{2,1,0:T(1,128)} %bitcast.3), calls=%async_computation | async-start | bytes 65536 | tf_op jit(solution)/shard_map/all_to_all | solution.py:51
  20.2 2.1 %fusion = f32[1024]{0:T(1024)S(1)} fusion(bf16[1024,1024]{1,0:T(8,128)(2,1)} %param.2), kind=kLoop, calls=%fused_computation.5 | loop fusion | flops 3144704 | bytes 2101248 | tf_op jit(solution)/shard_map/reduce_sum | solution.py:11
  22.3 0.0 copy-done
  22.3 8.3 %scatter_custom_fusion.1 = bf16[2048,1024]{1,0:T(8,128)(2,1)} fusion(s32[1024]{0:T(1024)S(1)} %bitcast.11, bf16[1024,1024]{1,0:T(8,128)(2,1)S(1)} %copy-done, f32[1024]{0:T(1024)S(1)} %add_rsqrt_fusion, bf16[]{:T(256)} %constant.11.clone.1), kind=kCustom, calls=%fused_computation.10 | custom fusion | flops 3145728 | bytes 6295554 | tf_op jit(solution)/shard_map/scatter | solution.py:44
  30.6 0.0 all-to-all-done
  30.6 10.5 %all-to-all-start.1 = ((bf16[64,32,1024]{2,1,0:T(8,128)(2,1)}), bf16[64,32,1024]{2,1,0:T(8,128)(2,1)}, u32[]{:S(2)}, u32[]{:S(2)}) async-start(bf16[64,32,1024]{2,1,0:T(8,128)(2,1)} %bitcast.9), calls=%async_computation.1 | async-start | bytes 8388608 | tf_op jit(solution)/shard_map/all_to_all | solution.py:50
  41.1 0.5 broadcast.40
  41.6 0.7 reduce.7
  42.3 0.1 broadcast_in_dim_reshape.4
  42.4 0.1 dynamic_slice.6
  42.5 94.5 %all-to-all-done.1 = bf16[64,32,1024]{2,1,0:T(8,128)(2,1)} async-done(((bf16[64,32,1024]{2,1,0:T(8,128)(2,1)}), bf16[64,32,1024]{2,1,0:T(8,128)(2,1)}, u32[]{:S(2)}, u32[]{:S(2)}) %all-to-all-start.1) | async-done | bytes 4194336 | tf_op jit(solution)/shard_map/all_to_all | solution.py:50
  137.0 5.1 %select_reduce_fusion = f32[512]{0:T(512)S(1)} fusion(bf16[2048,1024]{1,0:T(8,128)(2,1)} %bitcast.5, s32[2048]{0:T(1024)S(1)} %broadcast_in_dim_reshape.4, s32[512]{0:T(512)S(1)} %dynamic_slice.6, pred[2048]{0:T(1024)(128)(4,1)S(1)} %broadcast_compare_fusion, s32[]{:T(128)S(6)} %select_n.15), kind=kOutput, calls=%fused_computation.7 | convolution fusion | flops 2151677440 | bytes 5257220 | tf_op jit(solution)/shard_map/qd,kd->qk/dot_general | solution.py:20
  142.1 8.6 %all-gather = f32[4,1,512]{2,1,0:T(1,128)S(1)} all-gather(f32[1,1,512]{2,1,0:T(1,128)S(1)} %bitcast.15), channel_id=1, replica_groups=mesh['rows'=64,'help'=4] {'help'}, dimensions={0}, use_global_device_ids=true | all-gather | bytes 10240 | tf_op jit(solution)/shard_map/all_gather | solution.py:62
  150.7 0.7 all_to_all.18
  151.4 8.2 %all-to-all-start.2 = ((f32[64,1,32]{2,1,0:T(1,128)}), f32[64,1,32]{2,1,0:T(1,128)S(1)}, u32[]{:S(2)}, u32[]{:S(2)}) async-start(f32[64,1,32]{2,1,0:T(1,128)} %bitcast.7), calls=%async_computation.2 | async-start | bytes 65536 | tf_op jit(solution)/shard_map/all_to_all | solution.py:63
  159.6 9.3 %all-to-all-done.2 = f32[64,1,32]{2,1,0:T(1,128)S(1)} async-done(((f32[64,1,32]{2,1,0:T(1,128)}), f32[64,1,32]{2,1,0:T(1,128)S(1)}, u32[]{:S(2)}, u32[]{:S(2)}) %all-to-all-start.2) | async-done | bytes 8224 | tf_op jit(solution)/shard_map/all_to_all | solution.py:63
  168.9 0.5 broadcast.41
  169.4 0.7 reduce.8
  170.1 0.1 reshape.47
  170.2 10.5 %gather_fusion = f32[1024]{0:T(1024)} fusion(f32[2048]{0:T(1024)S(1)} %reshape.47, s32[1024]{0:T(1024)S(1)} %broadcast_clamp_fusion), kind=kCustom, calls=%fused_computation | custom fusion | bytes 12288 | tf_op jit(solution)/shard_map/gather | solution.py:66
  (6 shorter events, 0.1 us)
Async XLA Ops:
  0.0 22.3 %copy-start = (bf16[1024,1024]{1,0:T(8,128)(2,1)S(1)}, bf16[1024,1024]{1,0:T(8,128)(2,1)}, u32[]{:S(2)}) copy-start(bf16[1024,1024]{1,0:T(8,128)(2,1)} %param.2) | copy-start | bytes 6291460
  7.2 23.4 %all-to-all-start = ((s32[64,1,32]{2,1,0:T(1,128)}), s32[64,1,32]{2,1,0:T(1,128)S(1)}, u32[]{:S(2)}, u32[]{:S(2)}) async-start(s32[64,1,32]{2,1,0:T(1,128)} %bitcast.3), calls=%async_computation | async-start | bytes 65536 | tf_op jit(solution)/shard_map/all_to_all | solution.py:51
  30.6 106.4 %all-to-all-start.1 = ((bf16[64,32,1024]{2,1,0:T(8,128)(2,1)}), bf16[64,32,1024]{2,1,0:T(8,128)(2,1)}, u32[]{:S(2)}, u32[]{:S(2)}) async-start(bf16[64,32,1024]{2,1,0:T(8,128)(2,1)} %bitcast.9), calls=%async_computation.1 | async-start | bytes 8388608 | tf_op jit(solution)/shard_map/all_to_all | solution.py:50
  151.4 17.5 %all-to-all-start.2 = ((f32[64,1,32]{2,1,0:T(1,128)}), f32[64,1,32]{2,1,0:T(1,128)S(1)}, u32[]{:S(2)}, u32[]{:S(2)}) async-start(f32[64,1,32]{2,1,0:T(1,128)} %bitcast.7), calls=%async_computation.2 | async-start | bytes 65536 | tf_op jit(solution)/shard_map/all_to_all | solution.py:63
where the time goes:
time: 181 us
  waiting for transfers between devices  104 us (57%)
  starting transfers between devices  31.7 us (18%)
  local copies, waits for them, and re-layouts  17.5 us (10%)
  other arithmetic  12.6 us (7%)
  blocking collectives  8.6 us (5%)
  matrix products  6.58 us (4%)
    all_to_all x1, waiting for transfers between devices, local(): lax.all_to_all(send_rows, 'rows', split_axis=0, concat_axis=0, tiled=True)  94.5 us
    all_to_all x1, starting transfers between devices, local(): lax.all_to_all(send_ids, 'rows', split_axis=0, concat_axis=0, tiled=True)  13 us
    gather x1, local copies, waits for them, and re-layouts, local(): return returned.reshape(owners * most_rows)[slot_index]  10.5 us
    all_to_all x1, starting transfers between devices, local(): lax.all_to_all(send_rows, 'rows', split_axis=0, concat_axis=0, tiled=True)  10.5 us
    all_to_all x1, waiting for transfers between devices, local(): lax.all_to_all(everything.reshape(owners, most_rows), 'rows', split_axis=...  9.27 us
    all_gather x1, blocking collectives, local(): everything = lax.all_gather(best_rows, 'help', axis=0, tiled=True)  8.6 us
    scatter x1, other arithmetic, local(): send_rows = jnp.zeros((owners * most_rows, embeddings.shape[1]), jnp.bflo...  8.29 us
    all_to_all x1, starting transfers between devices, local(): lax.all_to_all(everything.reshape(owners, most_rows), 'rows', split_axis=...  8.18 us
  transfers between devices with their start and end apart: 3, of which 2 were waited for; matrix products, arithmetic and copies ran while one was open for 7% of the time, Pallas kernels for 0%

commit v1 on v0

v1 whole, which is shorter than its diff:
```python
import jax
import jax.numpy as jnp
from jax import lax
from jax.experimental import pallas as pl
from jax.experimental.pallas import tpu as pltpu
from jax.sharding import PartitionSpec as P

EPSILON = 1e-06
MESH = pl.DeviceIdType.MESH
D = 1024
ROWS = 1024
MOST = 32
NX, NZ, NY, NK = 4, 8, 4, 2
GROUP = NX * NK
BLOCK = GROUP * MOST
ORDER = (0, 1, 7, 2, 6, 3, 5, 4)
OWNERS = (0, 5)
FLAG = 4.0
OFF = -16.0


def kernel(emb_hbm, ids_ref, out_ref, emb, send, stage, keys, acc, row_bias, best_lane, ranks,
           onehot, best, ret1, ret2, ret3,
           emb_sem, z_send, z_recv, x_send, x_recv, x_copy, r1_send, r1_recv, r2_send, r2_recv,
           r3_send, r3_recv):
    r = lax.axis_index("rows")
    y = lax.axis_index("help")
    x, z, core = r // 16, (r // 2) % 8, r % 2
    lane_group = x * 2 + core

    def z_peer(offset):
        return {"rows": (x * 8 + (z + offset) % 8) * 2 + core}

    def x_peer(group):
        return {"rows": ((group // 2) * 8 + z) * 2 + group % 2}

    load = pltpu.make_async_copy(emb_hbm, emb, emb_sem)
    load.start()

    barrier = pltpu.get_barrier_semaphore()
    for offset in range(1, NZ):
        pl.semaphore_signal(barrier, inc=1, device_id=z_peer(offset), device_id_type=MESH)
    for step in range(1, GROUP):
        pl.semaphore_signal(
            barrier, inc=1, device_id=x_peer((lane_group + step) % GROUP), device_id_type=MESH
        )
    for step in range(1, NY):
        pl.semaphore_signal(
            barrier, inc=1, device_id={"help": (y + step) % NY}, device_id_type=MESH
        )

    iota_c = lax.broadcasted_iota(jnp.int32, (64, 128), 0)
    for b in range(8):
        hot = jnp.where(iota_c == ids_ref[b:b + 1, :], 1.0, 0.0).astype(jnp.bfloat16)
        onehot[b * 64:(b + 1) * 64, :] = hot
    tri_row = lax.broadcasted_iota(jnp.int32, (128, 256), 0)
    tri_col = lax.broadcasted_iota(jnp.int32, (128, 256), 1)
    tri = jnp.where((tri_row < tri_col) | (tri_col >= 128), 1.0, 0.0).astype(jnp.bfloat16)
    before = jnp.dot(onehot[...], tri, preferred_element_type=jnp.float32)
    base = jnp.zeros((64, 128), jnp.float32)
    for b in range(8):
        hot = onehot[b * 64:(b + 1) * 64, :].astype(jnp.float32)
        seen = before[b * 64:(b + 1) * 64, :128] + base
        rank = jnp.sum(hot * seen, axis=0, keepdims=True)
        ranks[b:b + 1, :] = rank.astype(jnp.int32)
        base = base + before[b * 64:(b + 1) * 64, 128:]
    best_lane[0:64, :] = base
    local_id = ids_ref[...] - 16 * y
    slot = (((local_id // 2) - z + 8) % 8) * 64 + (local_id % 2) * 32 + ranks[...]
    slot = jnp.where((local_id >= 0) & (local_id < 16), slot, -1)

    load.wait()
    iota_slot = lax.broadcasted_iota(jnp.int32, (64, 128), 0)
    lane = lax.broadcasted_iota(jnp.int32, (32, 128), 1)
    sub = lax.broadcasted_iota(jnp.int32, (32, 128), 0)

    def z_copy(offset):
        return pltpu.make_async_remote_copy(
            send.at[offset], stage.at[(8 - offset) % 8], z_send.at[offset],
            z_recv.at[(8 - offset) % 8], device_id=z_peer(offset), device_id_type=MESH
        )

    for half in range(2):
        offsets = ORDER[4 * half:4 * half + 4]
        pick = jnp.concatenate(
            [
                jnp.concatenate(
                    [
                        jnp.where(iota_slot + o * 64 == slot[b:b + 1, :], 1.0, 0.0).astype(jnp.bfloat16)
                        for b in range(8)
                    ],
                    axis=1,
                )
                for o in offsets
            ],
            axis=0,
        )
        picked = jnp.dot(pick, emb[...], preferred_element_type=jnp.float32)
        scale = lax.rsqrt(jnp.sum(picked * picked, axis=1, keepdims=True) + EPSILON)
        normed = (picked * scale).astype(jnp.bfloat16)
        for n, o in enumerate(offsets):
            send[o] = normed[n * 64:(n + 1) * 64, :]
            for j in range(2):
                cluster = 16 * y + ((z + o) % 8) * 2 + j
                count = best_lane[pl.ds(cluster, 1), :]
                empty = sub.astype(jnp.float32) >= count
                head = normed[n * 64 + j * 32:n * 64 + (j + 1) * 32, :128].astype(jnp.float32)
                head = jnp.where(empty & (lane == 0), FLAG, head)
                send[o, j * 32:(j + 1) * 32, 0:128] = head.astype(jnp.bfloat16)
        if half == 0:
            pl.semaphore_wait(barrier, NZ - 1 + GROUP - 1 + NY - 1)
        for o in offsets:
            if o:
                z_copy(o).start()

    def x_source(t, j):
        ref = send.at[0] if t == 0 else stage.at[ORDER[t]]
        return ref.at[pl.ds(j * 32, 32)]

    def x_target(t):
        return keys.at[t, pl.ds(pl.multiple_of(lane_group * 32, 32), 32)]

    def x_remote(t, j):
        return pltpu.make_async_remote_copy(
            x_source(t, j), x_target(t), x_send.at[t, j], x_recv.at[t],
            device_id=x_peer(OWNERS[j]), device_id_type=MESH
        )

    def x_local(t, j):
        return pltpu.make_async_copy(x_source(t, j), x_target(t), x_copy.at[t])

    def forward(t):
        if t:
            z_copy((8 - ORDER[t]) % 8).wait_recv()
        for j in range(2):
            @pl.when(lane_group == OWNERS[j])
            def _():
                x_local(t, j).start()

            @pl.when(lane_group != OWNERS[j])
            def _():
                x_remote(t, j).start()

    is_owner = (lane_group == OWNERS[0]) | (lane_group == OWNERS[1])
    lanes256 = lax.broadcasted_iota(jnp.int32, (1, 256), 1)
    dims = (((1,), (1,)), ((), ()))

    def compute(t):
        x_local(t, 0).wait()
        pltpu.make_async_remote_copy(
            keys.at[t, pl.ds(0, 224)], keys.at[t, pl.ds(0, 224)], x_send.at[0, 0], x_recv.at[t],
            device_id=x_peer(0), device_id_type=MESH
        ).wait_recv()
        new = keys[t]
        z_new = (z + ORDER[t]) % 8
        flags = keys[t, :, 0:128].astype(jnp.float32)
        bias = jnp.where(flags[:, 0:1] > 2.0, OFF, 0.0)
        row_bias[t] = jnp.broadcast_to(bias, (256, 128))
        first = jnp.where(lax.broadcasted_iota(jnp.int32, (16, 128), 1) == 0, 1.0, 0.0)
        lane_flag = lax.dot_general(
            first.astype(jnp.bfloat16), keys[t, :, 0:128], dims, preferred_element_type=jnp.float32
        )[0:1, :]
        lane_bias = jnp.where(lane_flag > 2.0, OFF, 0.0)
        scores = lax.dot_general(new, new, dims, preferred_element_type=jnp.float32)
        key_i = lax.broadcasted_iota(jnp.int32, (256, 256), 0)
        query_i = lax.broadcasted_iota(jnp.int32, (256, 256), 1)
        bias2 = jnp.concatenate([row_bias[t], row_bias[t]], axis=1)
        scores = jnp.where(key_i < query_i, scores + bias2, OFF)
        top = jnp.max(scores.reshape(32, 8, 256), axis=0)
        for u in range(t):
            z_old = (z + ORDER[u]) % 8
            shift = jnp.where(z_old < z_new, 0, 64)
            scores = lax.dot_general(keys[u], new, dims, preferred_element_type=jnp.float32)
            bias2 = jnp.concatenate([row_bias[u], row_bias[u]], axis=1)
            for g in range(4):
                new_later = lanes256 >= 64 * g + shift
                part = scores[64 * g:64 * (g + 1), :]
                down = part + bias2[64 * g:64 * (g + 1), :] + jnp.where(new_later, 0.0, OFF)
                top = jnp.maximum(top, jnp.max(down.reshape(8, 8, 256), axis=0))
                across = part + (lane_bias + jnp.where(new_later, OFF, 0.0))
                across = jnp.maximum(across[:, :128], across[:, 128:])
                rows = pl.ds(64 * g, 64)
                if u == t - 1:
                    acc[u, rows, :] = across
                else:
                    acc[u, rows, :] = jnp.maximum(acc[u, rows, :], across)
        best_lane[64 + t:65 + t, :] = jnp.max(top[:, :128], axis=0, keepdims=True)
        best_lane[72 + t:73 + t, :] = jnp.max(top[:, 128:], axis=0, keepdims=True)

    @pl.when(is_owner)
    def _():
        forward(0)
        for t in range(NZ):
            if t + 1 < NZ:
                forward(t + 1)
            compute(t)
        for h in range(2):
            for t in range(NZ):
                row = jnp.maximum(best_lane[64 + 8 * h + t:65 + 8 * h + t, :], -1.0)
                if t < NZ - 1:
                    turned = acc[t, h * 128:(h + 1) * 128, :].T
                    row = jnp.maximum(row, jnp.max(turned, axis=0, keepdims=True))
                best[h, t] = row

    @pl.when(jnp.logical_not(is_owner))
    def _():
        for t in range(NZ):
            forward(t)

    def back1(j, group):
        return pltpu.make_async_remote_copy(
            best.at[group // 4], ret1.at[j], r1_send.at[group], r1_recv.at[j],
            device_id=x_peer(group), device_id_type=MESH
        )

    for j in range(2):
        @pl.when(lane_group == OWNERS[j])
        def _():
            for group in range(GROUP):
                if group != OWNERS[j]:
                    back1(j, group).start()
            ret1[j] = best[OWNERS[j] // 4]

    for j in range(2):
        @pl.when(lane_group != OWNERS[j])
        def _():
            back1(j, 0).wait_recv()

    def back2(t):
        return pltpu.make_async_remote_copy(
            ret1.at[:, t], ret2.at[z], r2_send.at[t], r2_recv.at[(8 - ORDER[t]) % 8],
            device_id=z_peer(ORDER[t]), device_id_type=MESH
        )

    for t in range(1, NZ):
        back2(t).start()
    ret2[z] = ret1[:, 0]
    for t in range(1, NZ):
        pltpu.make_async_remote_copy(
            ret1.at[:, t], ret2.at[(z + ORDER[t]) % 8], r2_send.at[t], r2_recv.at[ORDER[t]],
            device_id=z_peer(ORDER[t]), device_id_type=MESH
        ).wait_recv()

    def back3(step):
        return pltpu.make_async_remote_copy(
            ret2, ret3.at[y], r3_send.at[step], r3_recv.at[(4 - step) % 4],
            device_id={"help": (y + step) % NY}, device_id_type=MESH
        )

    for step in range(1, NY):
        back3(step).start()
    ret3[y] = ret2[...]
    for step in range(1, NY):
        pltpu.make_async_remote_copy(
            ret2, ret3.at[(y + step) % NY], r3_send.at[step], r3_recv.at[step],
            device_id={"help": (y + step) % NY}, device_id_type=MESH
        ).wait_recv()

    values = ret3[...].reshape(64, 128)
    high = values.astype(jnp.bfloat16)
    rest = values - high.astype(jnp.float32)
    mid = rest.astype(jnp.bfloat16)
    low = (rest - mid.astype(jnp.float32)).astype(jnp.bfloat16)
    parts = jnp.concatenate([high, mid, low], axis=0)
    iota_lane = lax.broadcasted_iota(jnp.int32, (128, 128), 0)
    for b in range(8):
        hot = onehot[b * 64:(b + 1) * 64, :]
        hot3 = jnp.concatenate([hot, hot, hot], axis=0)
        table = lax.dot_general(
            parts, hot3, (((0,), (0,)), ((), ())), preferred_element_type=jnp.float32
        )
        want = ranks[b:b + 1, :] + (lane_group % 4) * 32
        out_ref[b:b + 1, :] = jnp.sum(jnp.where(iota_lane == want, table, 0.0), axis=0, keepdims=True)

    for offset in range(1, NZ):
        z_copy(offset).wait_send()
    for t in range(NZ):
        for j in range(2):
            @pl.when(lane_group != OWNERS[j])
            def _():
                x_remote(t, j).wait_send()
    for j in range(2):
        @pl.when(lane_group == OWNERS[j])
        def _():
            for group in range(GROUP):
                if group != OWNERS[j]:
                    back1(j, group).wait_send()
    for t in range(1, NZ):
        back2(t).wait_send()
    for step in range(1, NY):
        back3(step).wait_send()


def local(embeddings, clusters):
    dma = pltpu.SemaphoreType.DMA
    vmem = pltpu.VMEM
    out = pl.pallas_call(
        kernel,
        out_shape=jax.ShapeDtypeStruct((8, 128), jnp.float32),
        in_specs=[
            pl.BlockSpec(memory_space=pltpu.HBM),
            pl.BlockSpec(memory_space=pltpu.VMEM),
        ],
        out_specs=pl.BlockSpec(memory_space=pltpu.VMEM),
        scratch_shapes=[
            vmem((ROWS, D), jnp.bfloat16),
            vmem((NZ, 64, D), jnp.bfloat16),
            vmem((NZ, 64, D), jnp.bfloat16),
            vmem((NZ, BLOCK, D), jnp.bfloat16),
            vmem((NZ, BLOCK, 128), jnp.float32),
            vmem((NZ, BLOCK, 128), jnp.float32),
            vmem((80, 128), jnp.float32),
            vmem((8, 128), jnp.int32),
            vmem((512, 128), jnp.bfloat16),
            vmem((2, NZ, 1, 128), jnp.float32),
            vmem((2, NZ, 1, 128), jnp.float32),
            vmem((NZ, 2, 1, 128), jnp.float32),
            vmem((NY, NZ, 2, 1, 128), jnp.float32),
            dma,
            dma((NZ,)),
            dma((NZ,)),
            dma((NZ, 2)),
            dma((NZ,)),
            dma((NZ,)),
            dma((GROUP,)),
            dma((2,)),
            dma((NZ,)),
            dma((NZ,)),
            dma((NY,)),
            dma((NY,)),
        ],
        compiler_params=pltpu.CompilerParams(
            collective_id=0, has_side_effects=True, vmem_limit_bytes=48 << 20
        ),
    )(embeddings, clusters.reshape(8, 128))
    return out.reshape(ROWS)


def solution(mesh):
    placed = (P("rows", None), P("rows", None))
    return jax.shard_map(local, mesh=mesh, in_specs=placed, out_specs=P("rows"), check_vma=False)
```

time: 181 us -> 58.1 us (0.32)
  waiting for transfers between devices: 104 us -> 0 us
  Pallas kernels: 0 us -> 54.9 us
  starting transfers between devices: 31.7 us -> 0 us
  local copies, waits for them, and re-layouts: 17.5 us -> 2.87 us
  other arithmetic: 12.6 us -> 0 us
  blocking collectives: 8.6 us -> 0 us
  matrix products: 6.58 us -> 0 us
    all_to_all x3 -> x0, waiting for transfers between devices: 104 us -> none  [the longest x1 94.5 us: local(): lax.all_to_all(send_rows, 'rows', split_axis=0, concat_axis=0, tiled=True)]
    pallas_call x0 -> x1, Pallas kernels: none -> 54.9 us  [local(): pl.pallas_call(kernel, out_shape=jax.ShapeDtypeStruct((8, 128), jnp.float...]
    all_to_all x3 -> x0, starting transfers between devices: 31.7 us -> none  [the longest x1 13 us: local(): lax.all_to_all(send_ids, 'rows', split_axis=0, concat_axis=0, tiled=True)]
    gather x1 -> x0, local copies, waits for them, and re-layouts: 10.5 us -> none  [local(): return returned.reshape(owners * most_rows)[slot_index]]
    all_gather x1 -> x0, blocking collectives: 8.6 us -> none  [local(): everything = lax.all_gather(best_rows, 'help', axis=0, tiled=True)]
    scatter x1 -> x0, other arithmetic: 8.29 us -> none  [local(): send_rows = jnp.zeros((owners * most_rows, embeddings.shape[1]), jnp.bflo...]
    dot_general x2 -> x0, matrix products: 6.58 us -> none  [the longest x1 5.13 us: pair_scores(): jnp.einsum('qd,kd->qk', left_rows, right_rows, preferred_element_type=jnp...]
    scatter x1 -> x0, local copies, waits for them, and re-layouts: 4.32 us -> none  [local(): jnp.full((owners * most_rows,), -1, jnp.int32).at[slot_index]]
  transfers between devices with their start and end apart: 3 -> 0, of which waited for: 2 -> 0; matrix products, arithmetic and copies ran while one was open for 7% -> 0% of each run, Pallas kernels for 0% -> 0%
where the time goes in v1:
time: 58.1 us; the launch traced here: 57.8 us
  Pallas kernels  54.9 us (94%)
  local copies, waits for them, and re-layouts  2.87 us (5%)
    pallas_call x1, Pallas kernels, local(): pl.pallas_call(kernel, out_shape=jax.ShapeDtypeStruct((8, 128), jnp.float...  54.9 us
    unnamed x5, local copies, waits for them, and re-layouts  2.87 us

profile of v1, /device:TPU:1, one launch (start us, length us, event | category | flops | bytes accessed | tf_op | source)
XLA Modules:
  0.0 57.8 jit_solution(7335842336114351271)
XLA Ops:
  0.0 0.0 copy-start
  0.0 1.6 %copy-done = bf16[1024,1024]{1,0:T(8,128)(2,1)S(1)} copy-done((bf16[1024,1024]{1,0:T(8,128)(2,1)S(1)}, bf16[1024,1024]{1,0:T(8,128)(2,1)}, u32[]{:S(2)}) %copy-start) | copy-done | bytes 2097176
  1.6 0.0 copy-start.1
  1.6 0.7 %copy-done.1 = s32[1024,1]{0,1:T(1,128)S(1)} copy-done((s32[1024,1]{0,1:T(1,128)S(1)}, s32[1024,1]{0,1:T(1,128)}, u32[]{:S(2)}) %copy-start.1) | copy-done | bytes 4120
  2.3 54.9 %shard_map.28 = f32[8,128]{1,0:T(8,128)S(1)} custom-call(bf16[1024,1024]{1,0:T(8,128)(2,1)S(1)} %copy-done, s32[8,128]{1,0:T(8,128)S(1)} %bitcast.3), custom_call_target="tpu_custom_call" | custom-call | tf_op jit(solution)/shard_map/pallas_call | solution.py:297
  57.2 0.6 %copy.4 = f32[1024]{0:T(1024)} copy(f32[1024]{0:T(1024)S(1)} %bitcast.2) | data formatting | bytes 8192
Async XLA Ops:
  0.0 1.6 %copy-start = (bf16[1024,1024]{1,0:T(8,128)(2,1)S(1)}, bf16[1024,1024]{1,0:T(8,128)(2,1)}, u32[]{:S(2)}) copy-start(bf16[1024,1024]{1,0:T(8,128)(2,1)} %emb_hbm.1) | copy-start | bytes 6291460
  1.6 0.7 %copy-start.1 = (s32[1024,1]{0,1:T(1,128)S(1)}, s32[1024,1]{0,1:T(1,128)}, u32[]{:S(2)}) copy-start(s32[1024,1]{0,1:T(1,128)} %param.3) | copy-start | bytes 12292

commit v2 on v1

--- a/solution.py
+++ b/solution.py
@@ -20,9 +20,8 @@
 
 
 def kernel(emb_hbm, ids_ref, out_ref, emb, send, stage, keys, acc, row_bias, best_lane, ranks,
-           onehot, best, ret1, ret2, ret3,
-           emb_sem, z_send, z_recv, x_send, x_recv, x_copy, r1_send, r1_recv, r2_send, r2_recv,
-           r3_send, r3_recv):
+           onehot, best, table,
+           emb_sem, z_send, z_recv, x_send, x_recv, x_copy, back_send, back_recv):
     r = lax.axis_index("rows")
     y = lax.axis_index("help")
     x, z, core = r // 16, (r // 2) % 8, r % 2
@@ -200,63 +199,46 @@
                 if t < NZ - 1:
                     turned = acc[t, h * 128:(h + 1) * 128, :].T
                     row = jnp.maximum(row, jnp.max(turned, axis=0, keepdims=True))
-                best[h, t] = row
+                best[h, ORDER[t]] = row
 
     @pl.when(jnp.logical_not(is_owner))
     def _():
         for t in range(NZ):
             forward(t)
 
-    def back1(j, group):
+    def back(cluster, offset, step):
+        group = (lane_group + step) % GROUP
         return pltpu.make_async_remote_copy(
-            best.at[group // 4], ret1.at[j], r1_send.at[group], r1_recv.at[j],
-            device_id=x_peer(group), device_id_type=MESH
+            best.at[group // 4, offset], table.at[cluster], back_send, back_recv,
+            device_id={
+                "rows": ((group // 2) * 8 + (z + offset) % 8) * 2 + group % 2,
+                "help": (y + 2 - step // GROUP + NY) % NY,
+            },
+            device_id_type=MESH,
         )
 
     for j in range(2):
         @pl.when(lane_group == OWNERS[j])
         def _():
-            for group in range(GROUP):
-                if group != OWNERS[j]:
-                    back1(j, group).start()
-            ret1[j] = best[OWNERS[j] // 4]
-
-    for j in range(2):
-        @pl.when(lane_group != OWNERS[j])
-        def _():
-            back1(j, 0).wait_recv()
-
-    def back2(t):
-        return pltpu.make_async_remote_copy(
-            ret1.at[:, t], ret2.at[z], r2_send.at[t], r2_recv.at[(8 - ORDER[t]) % 8],
-            device_id=z_peer(ORDER[t]), device_id_type=MESH
-        )
-
-    for t in range(1, NZ):
-        back2(t).start()
-    ret2[z] = ret1[:, 0]
-    for t in range(1, NZ):
+            cluster = 16 * y + 2 * z + j
+            for offset in (4, 3, 5, 2, 6, 1, 7, 0):
+                for step in range(32):
+                    if step != 16 or offset != 0:
+                        back(cluster, offset, step).start()
+            table[cluster] = best[OWNERS[j] // 4, 0]
+            pltpu.make_async_remote_copy(
+                table.at[pl.ds(0, 63)], table.at[pl.ds(0, 63)], back_send, back_recv,
+                device_id=x_peer(0), device_id_type=MESH
+            ).wait_recv()
+
+    @pl.when(jnp.logical_not(is_owner))
+    def _():
         pltpu.make_async_remote_copy(
-            ret1.at[:, t], ret2.at[(z + ORDER[t]) % 8], r2_send.at[t], r2_recv.at[ORDER[t]],
-            device_id=z_peer(ORDER[t]), device_id_type=MESH
+            table.at[pl.ds(0, 64)], table.at[pl.ds(0, 64)], back_send, back_recv,
+            device_id=x_peer(0), device_id_type=MESH
         ).wait_recv()
 
-    def back3(step):
-        return pltpu.make_async_remote_copy(
-            ret2, ret3.at[y], r3_send.at[step], r3_recv.at[(4 - step) % 4],
-            device_id={"help": (y + step) % NY}, device_id_type=MESH
-        )
-
-    for step in range(1, NY):
-        back3(step).start()
-    ret3[y] = ret2[...]
-    for step in range(1, NY):
-        pltpu.make_async_remote_copy(
-            ret2, ret3.at[(y + step) % NY], r3_send.at[step], r3_recv.at[step],
-            device_id={"help": (y + step) % NY}, device_id_type=MESH
-        ).wait_recv()
-
-    values = ret3[...].reshape(64, 128)
+    values = table[0:64].reshape(64, 128)
     high = values.astype(jnp.bfloat16)
     rest = values - high.astype(jnp.float32)
     mid = rest.astype(jnp.bfloat16)
@@ -266,11 +248,11 @@
     for b in range(8):
         hot = onehot[b * 64:(b + 1) * 64, :]
         hot3 = jnp.concatenate([hot, hot, hot], axis=0)
-        table = lax.dot_general(
+        looked = lax.dot_general(
             parts, hot3, (((0,), (0,)), ((), ())), preferred_element_type=jnp.float32
         )
         want = ranks[b:b + 1, :] + (lane_group % 4) * 32
-        out_ref[b:b + 1, :] = jnp.sum(jnp.where(iota_lane == want, table, 0.0), axis=0, keepdims=True)
+        out_ref[b:b + 1, :] = jnp.sum(jnp.where(iota_lane == want, looked, 0.0), axis=0, keepdims=True)
 
     for offset in range(1, NZ):
         z_copy(offset).wait_send()
@@ -279,16 +261,12 @@
             @pl.when(lane_group != OWNERS[j])
             def _():
                 x_remote(t, j).wait_send()
-    for j in range(2):
-        @pl.when(lane_group == OWNERS[j])
-        def _():
-            for group in range(GROUP):
-                if group != OWNERS[j]:
-                    back1(j, group).wait_send()
-    for t in range(1, NZ):
-        back2(t).wait_send()
-    for step in range(1, NY):
-        back3(step).wait_send()
+    @pl.when(is_owner)
+    def _():
+        pltpu.make_async_remote_copy(
+            table.at[pl.ds(0, 255)], table.at[pl.ds(0, 255)], back_send, back_recv,
+            device_id=x_peer(0), device_id_type=MESH
+        ).wait_send()
 
 
 def local(embeddings, clusters):
@@ -313,24 +291,18 @@
             vmem((8, 128), jnp.int32),
             vmem((512, 128), jnp.bfloat16),
             vmem((2, NZ, 1, 128), jnp.float32),
-            vmem((2, NZ, 1, 128), jnp.float32),
-            vmem((NZ, 2, 1, 128), jnp.float32),
-            vmem((NY, NZ, 2, 1, 128), jnp.float32),
+            vmem((256, 1, 128), jnp.float32),
             dma,
             dma((NZ,)),
             dma((NZ,)),
             dma((NZ, 2)),
             dma((NZ,)),
             dma((NZ,)),
-            dma((GROUP,)),
-            dma((2,)),
-            dma((NZ,)),
-            dma((NZ,)),
-            dma((NY,)),
-            dma((NY,)),
+            dma,
+            dma,
         ],
         compiler_params=pltpu.CompilerParams(
-            collective_id=0, has_side_effects=True, vmem_limit_bytes=48 << 20
+            collective_id=0, has_side_effects=True, vmem_limit_bytes=60 << 20
         ),
     )(embeddings, clusters.reshape(8, 128))
     return out.reshape(ROWS)

time: 58.1 us -> 55 us (0.947)
  local copies, waits for them, and re-layouts: 2.87 us -> 1.28 us
  Pallas kernels: 54.9 us -> 53.6 us
    unnamed x5 -> x1, local copies, waits for them, and re-layouts: 2.87 us -> 1.28 us
    pallas_call x1, Pallas kernels: 54.9 us -> 53.6 us  [local(): pl.pallas_call(kernel, out_shape=jax.ShapeDtypeStruct((8, 128), jnp.float...]
where the time goes in v2:
time: 55 us; the launch traced here: 54.9 us
  Pallas kernels  53.6 us (97%)
  local copies, waits for them, and re-layouts  1.28 us (2%)
    pallas_call x1, Pallas kernels, local(): pl.pallas_call(kernel, out_shape=jax.ShapeDtypeStruct((8, 128), jnp.float...  53.6 us
    unnamed x1, local copies, waits for them, and re-layouts  1.28 us

profile of v2, /device:TPU:1, one launch (start us, length us, event | category | flops | bytes accessed | tf_op | source)
XLA Modules:
  0.0 54.9 jit_solution(15051125465183773435)
XLA Ops:
  0.0 53.6 %shard_map.28 = f32[8,128]{1,0:T(8,128)} custom-call(bf16[1024,1024]{1,0:T(8,128)(2,1)} %emb_hbm.1, s32[8,128]{1,0:T(8,128)} %bitcast.3), custom_call_target="tpu_custom_call" | custom-call | tf_op jit(solution)/shard_map/pallas_call | solution.py:275
  53.6 1.3 %copy.4 = f32[1024]{0:T(1024)} copy(f32[1024]{0:T(1024)} %bitcast.2) | data formatting | bytes 8192

commit v3 on v2

--- a/solution.py
+++ b/solution.py
@@ -14,35 +14,52 @@
 GROUP = NX * NK
 BLOCK = GROUP * MOST
 ORDER = (0, 1, 7, 2, 6, 3, 5, 4)
-OWNERS = (0, 5)
 FLAG = 4.0
 OFF = -16.0
 
 
-def kernel(emb_hbm, ids_ref, out_ref, emb, send, stage, keys, acc, row_bias, best_lane, ranks,
+def kernel(emb_hbm, ids_ref, out_ref, emb, send, keys, acc, row_bias, best_lane, ranks,
            onehot, best, table,
-           emb_sem, z_send, z_recv, x_send, x_recv, x_copy, back_send, back_recv):
+           emb_sem, out_sem, in_sem, own_sem, back_send, back_recv):
     r = lax.axis_index("rows")
     y = lax.axis_index("help")
     x, z, core = r // 16, (r // 2) % 8, r % 2
     lane_group = x * 2 + core
 
-    def z_peer(offset):
-        return {"rows": (x * 8 + (z + offset) % 8) * 2 + core}
-
-    def x_peer(group):
-        return {"rows": ((group // 2) * 8 + z) * 2 + group % 2}
+    side = (y + 3 - 2 * core) % NY
+
+    def owner_core(x_owner):
+        return x_owner // 2
+
+    is_owner = ((x + y + z) % 2 == 0) & (core == owner_core(x))
+
+    def device(x_to, z_to, core_to, y_to):
+        return {"rows": (x_to * 8 + z_to) * 2 + core_to, "help": y_to}
 
     load = pltpu.make_async_copy(emb_hbm, emb, emb_sem)
     load.start()
 
     barrier = pltpu.get_barrier_semaphore()
-    for offset in range(1, NZ):
-        pl.semaphore_signal(barrier, inc=1, device_id=z_peer(offset), device_id_type=MESH)
-    for step in range(1, GROUP):
-        pl.semaphore_signal(
-            barrier, inc=1, device_id=x_peer((lane_group + step) % GROUP), device_id_type=MESH
-        )
+    @pl.when(is_owner)
+    def _():
+        for offset in (4, 3, 5, 2, 6, 1, 7, 0):
+            z_to = (z + offset) % 8
+            for step in range(NX):
+                x_to = (x + 2 + step) % NX
+                for core_to in range(NK):
+                    @pl.when((offset != 0) | (step != 2) | (core_to != core))
+                    def _():
+                        pl.semaphore_signal(
+                            barrier, inc=1, device_id=device(x_to, z_to, core_to, y),
+                            device_id_type=MESH
+                        )
+
+                    pl.semaphore_signal(
+                        barrier, inc=1,
+                        device_id=device(x_to, z_to, core_to, (y + 1 + 2 * core_to) % NY),
+                        device_id_type=MESH
+                    )
+
     for step in range(1, NY):
         pl.semaphore_signal(
             barrier, inc=1, device_id={"help": (y + step) % NY}, device_id_type=MESH
@@ -64,20 +81,36 @@
         ranks[b:b + 1, :] = rank.astype(jnp.int32)
         base = base + before[b * 64:(b + 1) * 64, 128:]
     best_lane[0:64, :] = base
-    local_id = ids_ref[...] - 16 * y
-    slot = (((local_id // 2) - z + 8) % 8) * 64 + (local_id % 2) * 32 + ranks[...]
-    slot = jnp.where((local_id >= 0) & (local_id < 16), slot, -1)
+    ids = ids_ref[...]
+    plane, z_to, x_to = ids // 16, (ids // 2) % 8, (ids % 2) * 2 + (ids // 2 + ids // 16) % 2
+    low = ranks[...] < 16
+    slot = ((z_to - z + 8) % 8) * 64 + ((x_to - x + 4) % 4) * 16 + ranks[...] % 16
+    slot = jnp.where(plane == jnp.where(low, y, side), slot, -1)
 
     load.wait()
     iota_slot = lax.broadcasted_iota(jnp.int32, (64, 128), 0)
-    lane = lax.broadcasted_iota(jnp.int32, (32, 128), 1)
-    sub = lax.broadcasted_iota(jnp.int32, (32, 128), 0)
-
-    def z_copy(offset):
+    lane = lax.broadcasted_iota(jnp.int32, (16, 128), 1)
+    sub = lax.broadcasted_iota(jnp.int32, (16, 128), 0)
+
+    def place(offset, step):
+        z_to, x_to = (z + offset) % 8, (x + step) % NX
+        here = (x_to + y + z_to) % 2 == 0
+        return z_to, x_to, here, jnp.where(here, y, side)
+
+    def target(offset, here):
+        start = pl.multiple_of(lane_group * 32 + jnp.where(here, 0, 16), 16)
+        return keys.at[ORDER.index((8 - offset) % 8), pl.ds(start, 16)]
+
+    def send_copy(offset, step):
+        z_to, x_to, here, y_to = place(offset, step)
         return pltpu.make_async_remote_copy(
-            send.at[offset], stage.at[(8 - offset) % 8], z_send.at[offset],
-            z_recv.at[(8 - offset) % 8], device_id=z_peer(offset), device_id_type=MESH
-        )
+            send.at[offset, pl.ds(step * 16, 16)], target(offset, here), out_sem.at[offset],
+            in_sem.at[ORDER.index((8 - offset) % 8)],
+            device_id=device(x_to, z_to, owner_core(x_to), y_to), device_id_type=MESH
+        )
+
+    def own_copy():
+        return pltpu.make_async_copy(send.at[0, pl.ds(0, 16)], target(0, True), own_sem)
 
     for half in range(2):
         offsets = ORDER[4 * half:4 * half + 4]
@@ -99,56 +132,46 @@
         normed = (picked * scale).astype(jnp.bfloat16)
         for n, o in enumerate(offsets):
             send[o] = normed[n * 64:(n + 1) * 64, :]
-            for j in range(2):
-                cluster = 16 * y + ((z + o) % 8) * 2 + j
-                count = best_lane[pl.ds(cluster, 1), :]
-                empty = sub.astype(jnp.float32) >= count
-                head = normed[n * 64 + j * 32:n * 64 + (j + 1) * 32, :128].astype(jnp.float32)
+            for step in range(NX):
+                z_to, x_to, here, y_to = place(o, step)
+                count = best_lane[pl.ds(16 * y_to + 2 * z_to + x_to // 2, 1), :]
+                empty = (sub + jnp.where(here, 0, 16)).astype(jnp.float32) >= count
+                first = n * 64 + step * 16
+                head = normed[first:first + 16, :128].astype(jnp.float32)
                 head = jnp.where(empty & (lane == 0), FLAG, head)
-                send[o, j * 32:(j + 1) * 32, 0:128] = head.astype(jnp.bfloat16)
+                send[o, step * 16:(step + 1) * 16, 0:128] = head.astype(jnp.bfloat16)
         if half == 0:
-            pl.semaphore_wait(barrier, NZ - 1 + GROUP - 1 + NY - 1)
+            @pl.when(is_owner)
+            def _():
+                pl.semaphore_wait(barrier, 31 + NY - 1)
+
+            @pl.when(jnp.logical_not(is_owner))
+            def _():
+                pl.semaphore_wait(barrier, 32 + NY - 1)
         for o in offsets:
+            for step in range(1, NX):
+                send_copy(o, step).start()
             if o:
-                z_copy(o).start()
-
-    def x_source(t, j):
-        ref = send.at[0] if t == 0 else stage.at[ORDER[t]]
-        return ref.at[pl.ds(j * 32, 32)]
-
-    def x_target(t):
-        return keys.at[t, pl.ds(pl.multiple_of(lane_group * 32, 32), 32)]
-
-    def x_remote(t, j):
-        return pltpu.make_async_remote_copy(
-            x_source(t, j), x_target(t), x_send.at[t, j], x_recv.at[t],
-            device_id=x_peer(OWNERS[j]), device_id_type=MESH
-        )
-
-    def x_local(t, j):
-        return pltpu.make_async_copy(x_source(t, j), x_target(t), x_copy.at[t])
-
-    def forward(t):
-        if t:
-            z_copy((8 - ORDER[t]) % 8).wait_recv()
-        for j in range(2):
-            @pl.when(lane_group == OWNERS[j])
-            def _():
-                x_local(t, j).start()
-
-            @pl.when(lane_group != OWNERS[j])
-            def _():
-                x_remote(t, j).start()
-
-    is_owner = (lane_group == OWNERS[0]) | (lane_group == OWNERS[1])
+                send_copy(o, 0).start()
+            else:
+                @pl.when(is_owner)
+                def _():
+                    own_copy().start()
+
+                @pl.when(jnp.logical_not(is_owner))
+                def _():
+                    send_copy(0, 0).start()
+
     lanes256 = lax.broadcasted_iota(jnp.int32, (1, 256), 1)
     dims = (((1,), (1,)), ((), ()))
 
     def compute(t):
-        x_local(t, 0).wait()
-        pltpu.make_async_remote_copy(
-            keys.at[t, pl.ds(0, 224)], keys.at[t, pl.ds(0, 224)], x_send.at[0, 0], x_recv.at[t],
-            device_id=x_peer(0), device_id_type=MESH
+        if t == 0:
+            own_copy().wait()
+        rows = pl.ds(0, 240 if t == 0 else 256)
+        pltpu.make_async_remote_copy(
+            keys.at[t, rows], keys.at[t, rows], out_sem.at[0], in_sem.at[t],
+            device_id=device(x, z, 1 - core, y), device_id_type=MESH
         ).wait_recv()
         new = keys[t]
         z_new = (z + ORDER[t]) % 8
@@ -188,10 +211,7 @@
 
     @pl.when(is_owner)
     def _():
-        forward(0)
         for t in range(NZ):
-            if t + 1 < NZ:
-                forward(t + 1)
             compute(t)
         for h in range(2):
             for t in range(NZ):
@@ -200,11 +220,6 @@
                     turned = acc[t, h * 128:(h + 1) * 128, :].T
                     row = jnp.maximum(row, jnp.max(turned, axis=0, keepdims=True))
                 best[h, ORDER[t]] = row
-
-    @pl.when(jnp.logical_not(is_owner))
-    def _():
-        for t in range(NZ):
-            forward(t)
 
     def back(cluster, offset, step):
         group = (lane_group + step) % GROUP
@@ -217,25 +232,24 @@
             device_id_type=MESH,
         )
 
-    for j in range(2):
-        @pl.when(lane_group == OWNERS[j])
-        def _():
-            cluster = 16 * y + 2 * z + j
-            for offset in (4, 3, 5, 2, 6, 1, 7, 0):
-                for step in range(32):
-                    if step != 16 or offset != 0:
-                        back(cluster, offset, step).start()
-            table[cluster] = best[OWNERS[j] // 4, 0]
-            pltpu.make_async_remote_copy(
-                table.at[pl.ds(0, 63)], table.at[pl.ds(0, 63)], back_send, back_recv,
-                device_id=x_peer(0), device_id_type=MESH
-            ).wait_recv()
+    @pl.when(is_owner)
+    def _():
+        cluster = 16 * y + 2 * z + x // 2
+        for offset in (4, 3, 5, 2, 6, 1, 7, 0):
+            for step in range(32):
+                if step != 16 or offset != 0:
+                    back(cluster, offset, step).start()
+        table[cluster] = best[lane_group // 4, 0]
+        pltpu.make_async_remote_copy(
+            table.at[pl.ds(0, 63)], table.at[pl.ds(0, 63)], back_send, back_recv,
+            device_id=device(x, z, 1 - core, y), device_id_type=MESH
+        ).wait_recv()
 
     @pl.when(jnp.logical_not(is_owner))
     def _():
         pltpu.make_async_remote_copy(
             table.at[pl.ds(0, 64)], table.at[pl.ds(0, 64)], back_send, back_recv,
-            device_id=x_peer(0), device_id_type=MESH
+            device_id=device(x, z, 1 - core, y), device_id_type=MESH
         ).wait_recv()
 
     values = table[0:64].reshape(64, 128)
@@ -254,18 +268,29 @@
         want = ranks[b:b + 1, :] + (lane_group % 4) * 32
         out_ref[b:b + 1, :] = jnp.sum(jnp.where(iota_lane == want, looked, 0.0), axis=0, keepdims=True)
 
+    def sent(offset, rows):
+        part = keys.at[0, pl.ds(0, rows)]
+        pltpu.make_async_remote_copy(
+            part, part, out_sem.at[offset], in_sem.at[0], device_id=device(x, z, 1 - core, y),
+            device_id_type=MESH
+        ).wait_send()
+
     for offset in range(1, NZ):
-        z_copy(offset).wait_send()
-    for t in range(NZ):
-        for j in range(2):
-            @pl.when(lane_group != OWNERS[j])
-            def _():
-                x_remote(t, j).wait_send()
+        sent(offset, 64)
+
+    @pl.when(jnp.logical_not(is_owner))
+    def _():
+        sent(0, 64)
+
+    @pl.when(is_owner)
+    def _():
+        sent(0, 48)
+
     @pl.when(is_owner)
     def _():
         pltpu.make_async_remote_copy(
             table.at[pl.ds(0, 255)], table.at[pl.ds(0, 255)], back_send, back_recv,
-            device_id=x_peer(0), device_id_type=MESH
+            device_id=device(x, z, 1 - core, y), device_id_type=MESH
         ).wait_send()
 
 
@@ -283,7 +308,6 @@
         scratch_shapes=[
             vmem((ROWS, D), jnp.bfloat16),
             vmem((NZ, 64, D), jnp.bfloat16),
-            vmem((NZ, 64, D), jnp.bfloat16),
             vmem((NZ, BLOCK, D), jnp.bfloat16),
             vmem((NZ, BLOCK, 128), jnp.float32),
             vmem((NZ, BLOCK, 128), jnp.float32),
@@ -295,9 +319,7 @@
             dma,
             dma((NZ,)),
             dma((NZ,)),
-            dma((NZ, 2)),
-            dma((NZ,)),
-            dma((NZ,)),
+            dma,
             dma,
             dma,
         ],

time: 55 us -> 50.9 us (0.925)
  Pallas kernels: 53.6 us -> 49.5 us
    pallas_call x1, Pallas kernels: 53.6 us -> 49.5 us  [local(): pl.pallas_call(kernel, out_shape=jax.ShapeDtypeStruct((8, 128), jnp.float...]
where the time goes in v3:
time: 50.9 us; the launch traced here: 50.7 us
  Pallas kernels  49.5 us (97%)
  local copies, waits for them, and re-layouts  1.28 us (3%)
    pallas_call x1, Pallas kernels, local(): pl.pallas_call(kernel, out_shape=jax.ShapeDtypeStruct((8, 128), jnp.float...  49.5 us
    unnamed x1, local copies, waits for them, and re-layouts  1.28 us

profile of v3, /device:TPU:1, one launch (start us, length us, event | category | flops | bytes accessed | tf_op | source)
XLA Modules:
  0.0 50.7 jit_solution(16639001457380846045)
XLA Ops:
  0.0 49.5 %shard_map.28 = f32[8,128]{1,0:T(8,128)} custom-call(bf16[1024,1024]{1,0:T(8,128)(2,1)} %emb_hbm.1, s32[8,128]{1,0:T(8,128)} %bitcast.3), custom_call_target="tpu_custom_call" | custom-call | tf_op jit(solution)/shard_map/pallas_call | solution.py:300
  49.5 1.3 %copy.4 = f32[1024]{0:T(1024)} copy(f32[1024]{0:T(1024)} %bitcast.2) | data formatting | bytes 8192

commit v4 on v3

--- a/solution.py
+++ b/solution.py
@@ -219,27 +219,25 @@
                 if t < NZ - 1:
                     turned = acc[t, h * 128:(h + 1) * 128, :].T
                     row = jnp.maximum(row, jnp.max(turned, axis=0, keepdims=True))
-                best[h, ORDER[t]] = row
-
-    def back(cluster, offset, step):
-        group = (lane_group + step) % GROUP
+                best[h, (z + ORDER[t]) % 8] = row
+
+    def back(cluster, group, z_to, y_to):
         return pltpu.make_async_remote_copy(
-            best.at[group // 4, offset], table.at[cluster], back_send, back_recv,
-            device_id={
-                "rows": ((group // 2) * 8 + (z + offset) % 8) * 2 + group % 2,
-                "help": (y + 2 - step // GROUP + NY) % NY,
-            },
-            device_id_type=MESH,
+            best.at[group // 4, z_to], table.at[cluster], back_send, back_recv,
+            device_id=device(group // 2, z_to, group % 2, y_to), device_id_type=MESH
         )
 
     @pl.when(is_owner)
     def _():
         cluster = 16 * y + 2 * z + x // 2
-        for offset in (4, 3, 5, 2, 6, 1, 7, 0):
-            for step in range(32):
-                if step != 16 or offset != 0:
-                    back(cluster, offset, step).start()
-        table[cluster] = best[lane_group // 4, 0]
+        for z_to in range(NZ):
+            for y_to in range(NY):
+                for group in range(GROUP):
+                    @pl.when((lane_group != group) | (z != z_to) | (y != y_to))
+                    def _():
+                        back(cluster, group, z_to, y_to).start()
+
+        table[cluster] = best[lane_group // 4, z]
         pltpu.make_async_remote_copy(
             table.at[pl.ds(0, 63)], table.at[pl.ds(0, 63)], back_send, back_recv,
             device_id=device(x, z, 1 - core, y), device_id_type=MESH
@@ -324,7 +322,7 @@
             dma,
         ],
         compiler_params=pltpu.CompilerParams(
-            collective_id=0, has_side_effects=True, vmem_limit_bytes=60 << 20
+            collective_id=0, has_side_effects=True, vmem_limit_bytes=52 << 20
         ),
     )(embeddings, clusters.reshape(8, 128))
     return out.reshape(ROWS)

time: 50.9 us -> 48.3 us (0.949)
  Pallas kernels: 49.5 us -> 46.9 us
    pallas_call x1, Pallas kernels: 49.5 us -> 46.9 us  [local(): pl.pallas_call(kernel, out_shape=jax.ShapeDtypeStruct((8, 128), jnp.float...]
    unnamed x1 -> x3, local copies, waits for them, and re-layouts: 1.28 us -> 1.28 us
where the time goes in v4:
time: 48.3 us; the launch traced here: 48.2 us
  Pallas kernels  46.9 us (97%)
  local copies, waits for them, and re-layouts  1.28 us (3%)
    pallas_call x1, Pallas kernels, local(): pl.pallas_call(kernel, out_shape=jax.ShapeDtypeStruct((8, 128), jnp.float...  46.9 us
    unnamed x3, local copies, waits for them, and re-layouts  1.28 us

profile of v4, /device:TPU:1, one launch (start us, length us, event | category | flops | bytes accessed | tf_op | source)
XLA Modules:
  0.0 48.2 jit_solution(17375766678505002776)
XLA Ops:
  0.0 0.0 copy-start
  0.0 0.7 %copy-done = s32[1024,1]{0,1:T(1,128)S(1)} copy-done((s32[1024,1]{0,1:T(1,128)S(1)}, s32[1024,1]{0,1:T(1,128)}, u32[]{:S(2)}) %copy-start) | copy-done | bytes 4120
  0.7 46.9 %shard_map.28 = f32[8,128]{1,0:T(8,128)S(1)} custom-call(bf16[1024,1024]{1,0:T(8,128)(2,1)} %emb_hbm.1, s32[8,128]{1,0:T(8,128)S(1)} %bitcast.3), custom_call_target="tpu_custom_call" | custom-call | tf_op jit(solution)/shard_map/pallas_call | solution.py:298
  47.6 0.6 %copy.4 = f32[1024]{0:T(1024)} copy(f32[1024]{0:T(1024)S(1)} %bitcast.2) | data formatting | bytes 8192
Async XLA Ops:
  0.0 0.7 %copy-start = (s32[1024,1]{0,1:T(1,128)S(1)}, s32[1024,1]{0,1:T(1,128)}, u32[]{:S(2)}) copy-start(s32[1024,1]{0,1:T(1,128)} %param.3) | copy-start | bytes 12292

commit v5 on v4

--- a/solution.py
+++ b/solution.py
@@ -14,11 +14,12 @@
 GROUP = NX * NK
 BLOCK = GROUP * MOST
 ORDER = (0, 1, 7, 2, 6, 3, 5, 4)
+VMEM_LIMIT = 56553472
 FLAG = 4.0
 OFF = -16.0
 
 
-def kernel(emb_hbm, ids_ref, out_ref, emb, send, keys, acc, row_bias, best_lane, ranks,
+def kernel(emb_hbm, ids_hbm, out_ref, ids_ref, emb, send, keys, acc, row_bias, best_lane, ranks,
            onehot, best, table,
            emb_sem, out_sem, in_sem, own_sem, back_send, back_recv):
     r = lax.axis_index("rows")
@@ -38,33 +39,33 @@
 
     load = pltpu.make_async_copy(emb_hbm, emb, emb_sem)
     load.start()
+    load_ids = pltpu.make_async_copy(ids_hbm, ids_ref, own_sem)
+    load_ids.start()
 
     barrier = pltpu.get_barrier_semaphore()
-    @pl.when(is_owner)
-    def _():
-        for offset in (4, 3, 5, 2, 6, 1, 7, 0):
-            z_to = (z + offset) % 8
-            for step in range(NX):
-                x_to = (x + 2 + step) % NX
-                for core_to in range(NK):
-                    @pl.when((offset != 0) | (step != 2) | (core_to != core))
-                    def _():
-                        pl.semaphore_signal(
-                            barrier, inc=1, device_id=device(x_to, z_to, core_to, y),
-                            device_id_type=MESH
-                        )
-
-                    pl.semaphore_signal(
-                        barrier, inc=1,
-                        device_id=device(x_to, z_to, core_to, (y + 1 + 2 * core_to) % NY),
-                        device_id_type=MESH
-                    )
-
     for step in range(1, NY):
         pl.semaphore_signal(
             barrier, inc=1, device_id={"help": (y + step) % NY}, device_id_type=MESH
         )
 
+    @pl.when(is_owner)
+    def _():
+        def ready(x_to, z_to, core_to, y_to):
+            pl.semaphore_signal(
+                barrier, inc=1, device_id=device(x_to, z_to, core_to, y_to), device_id_type=MESH
+            )
+
+        for offset in (4, 3, 5, 2, 6, 1, 7, 0):
+            z_to = (z + offset) % 8
+            for step in (2, 1, 3, 0):
+                x_to = (x + step) % NX
+                for core_to in range(NK):
+                    ready(x_to, z_to, core_to, (y + 1 + 2 * core_to) % NY)
+                    if offset or step:
+                        ready(x_to, z_to, core_to, y)
+        ready(x, z, 1 - core, y)
+
+    load_ids.wait()
     iota_c = lax.broadcasted_iota(jnp.int32, (64, 128), 0)
     for b in range(8):
         hot = jnp.where(iota_c == ids_ref[b:b + 1, :], 1.0, 0.0).astype(jnp.bfloat16)
@@ -112,8 +113,8 @@
     def own_copy():
         return pltpu.make_async_copy(send.at[0, pl.ds(0, 16)], target(0, True), own_sem)
 
-    for half in range(2):
-        offsets = ORDER[4 * half:4 * half + 4]
+    for half in range(1):
+        offsets = ORDER
         pick = jnp.concatenate(
             [
                 jnp.concatenate(
@@ -230,12 +231,13 @@
     @pl.when(is_owner)
     def _():
         cluster = 16 * y + 2 * z + x // 2
-        for z_to in range(NZ):
-            for y_to in range(NY):
-                for group in range(GROUP):
-                    @pl.when((lane_group != group) | (z != z_to) | (y != y_to))
-                    def _():
-                        back(cluster, group, z_to, y_to).start()
+        me = (y * NZ + z) * GROUP + lane_group
+        places = [(z_to, y_to) for z_to in range(NZ) for y_to in range(NY)]
+        for z_to, y_to in sorted(places, key=lambda p: p[0] + (1.5 if p[1] else 0.0)):
+            for group in range(GROUP):
+                @pl.when(me != (y_to * NZ + z_to) * GROUP + group)
+                def _():
+                    back(cluster, group, z_to, y_to).start()
 
         table[cluster] = best[lane_group // 4, z]
         pltpu.make_async_remote_copy(
@@ -300,10 +302,11 @@
         out_shape=jax.ShapeDtypeStruct((8, 128), jnp.float32),
         in_specs=[
             pl.BlockSpec(memory_space=pltpu.HBM),
-            pl.BlockSpec(memory_space=pltpu.VMEM),
+            pl.BlockSpec(memory_space=pltpu.HBM),
         ],
         out_specs=pl.BlockSpec(memory_space=pltpu.VMEM),
         scratch_shapes=[
+            vmem((8, 128), jnp.int32),
             vmem((ROWS, D), jnp.bfloat16),
             vmem((NZ, 64, D), jnp.bfloat16),
             vmem((NZ, BLOCK, D), jnp.bfloat16),
@@ -322,7 +325,7 @@
             dma,
         ],
         compiler_params=pltpu.CompilerParams(
-            collective_id=0, has_side_effects=True, vmem_limit_bytes=52 << 20
+            collective_id=0, has_side_effects=True, vmem_limit_bytes=VMEM_LIMIT
         ),
     )(embeddings, clusters.reshape(8, 128))
     return out.reshape(ROWS)

time: 48.3 us -> 47.4 us (0.981)
  local copies, waits for them, and re-layouts: 1.28 us -> 0.6 us
    unnamed x3 -> x1, local copies, waits for them, and re-layouts: 1.28 us -> 0.6 us
where the time goes in v5:
time: 47.4 us; the launch traced here: 47.3 us
  Pallas kernels  46.7 us (99%)
  local copies, waits for them, and re-layouts  0.6 us (1%)
    pallas_call x1, Pallas kernels, local(): pl.pallas_call(kernel, out_shape=jax.ShapeDtypeStruct((8, 128), jnp.float...  46.7 us

profile of v5, /device:TPU:1, one launch (start us, length us, event | category | flops | bytes accessed | tf_op | source)
XLA Modules:
  0.0 47.3 jit_solution(2608117598044468818)
XLA Ops:
  0.0 46.7 %shard_map.28 = f32[8,128]{1,0:T(8,128)S(1)} custom-call(bf16[1024,1024]{1,0:T(8,128)(2,1)} %emb_hbm.1, s32[8,128]{1,0:T(8,128)} %bitcast.3), custom_call_target="tpu_custom_call" | custom-call | tf_op jit(solution)/shard_map/pallas_call | solution.py:300
  46.8 0.6 %copy.4 = f32[1024]{0:T(1024)} copy(f32[1024]{0:T(1024)S(1)} %bitcast.2) | data formatting | bytes 8192

commit v6 on v5

--- a/solution.py
+++ b/solution.py
@@ -20,7 +20,7 @@
 
 
 def kernel(emb_hbm, ids_hbm, out_ref, ids_ref, emb, send, keys, acc, row_bias, best_lane, ranks,
-           onehot, best, table,
+           onehot, best, head, table,
            emb_sem, out_sem, in_sem, own_sem, back_send, back_recv):
     r = lax.axis_index("rows")
     y = lax.axis_index("help")
@@ -138,9 +138,9 @@
                 count = best_lane[pl.ds(16 * y_to + 2 * z_to + x_to // 2, 1), :]
                 empty = (sub + jnp.where(here, 0, 16)).astype(jnp.float32) >= count
                 first = n * 64 + step * 16
-                head = normed[first:first + 16, :128].astype(jnp.float32)
-                head = jnp.where(empty & (lane == 0), FLAG, head)
-                send[o, step * 16:(step + 1) * 16, 0:128] = head.astype(jnp.bfloat16)
+                start = normed[first:first + 16, :128].astype(jnp.float32)
+                start = jnp.where(empty & (lane == 0), FLAG, start)
+                send[o, step * 16:(step + 1) * 16, 0:128] = start.astype(jnp.bfloat16)
         if half == 0:
             @pl.when(is_owner)
             def _():
@@ -165,6 +165,21 @@
 
     lanes256 = lax.broadcasted_iota(jnp.int32, (1, 256), 1)
     dims = (((1,), (1,)), ((), ()))
+
+    def back(cluster, group, z_to, y_to):
+        return pltpu.make_async_remote_copy(
+            best.at[group // 4, z_to], table.at[cluster], back_send, back_recv,
+            device_id=device(group // 2, z_to, group % 2, y_to), device_id_type=MESH
+        )
+
+    me = (y * NZ + z) * GROUP + lane_group
+    cluster = 16 * y + 2 * z + x // 2
+
+    def head_back(group, y_to):
+        return pltpu.make_async_remote_copy(
+            head.at[0], table.at[cluster], back_send, back_recv,
+            device_id=device(0, 0, group, y_to), device_id_type=MESH
+        )
 
     def compute(t):
         if t == 0:
@@ -190,6 +205,14 @@
         bias2 = jnp.concatenate([row_bias[t], row_bias[t]], axis=1)
         scores = jnp.where(key_i < query_i, scores + bias2, OFF)
         top = jnp.max(scores.reshape(32, 8, 256), axis=0)
+        if t == NZ - 1:
+            @pl.when(z_new == 0)
+            def _():
+                head[0] = jnp.maximum(jnp.max(top[:, :128], axis=0, keepdims=True), -1.0)
+                for y_to in range(NY):
+                    for group in range(NK):
+                        head_back(group, y_to).start()
+
         for u in range(t):
             z_old = (z + ORDER[u]) % 8
             shift = jnp.where(z_old < z_new, 0, 64)
@@ -213,6 +236,18 @@
     @pl.when(is_owner)
     def _():
         for t in range(NZ):
+            if t == NZ - 1:
+                @pl.when(z != NZ // 2)
+                def _():
+                    offset = (8 - z) % 8
+                    at = jnp.where(offset < 4, jnp.maximum(2 * offset - 1, 0), 2 * (8 - offset))
+                    head[0] = jnp.maximum(best_lane[pl.ds(64 + at, 1), :], -1.0)
+                    for y_to in range(NY):
+                        for group in range(NK):
+                            @pl.when(me != y_to * NZ * GROUP + group)
+                            def _():
+                                head_back(group, y_to).start()
+
             compute(t)
         for h in range(2):
             for t in range(NZ):
@@ -222,22 +257,15 @@
                     row = jnp.maximum(row, jnp.max(turned, axis=0, keepdims=True))
                 best[h, (z + ORDER[t]) % 8] = row
 
-    def back(cluster, group, z_to, y_to):
-        return pltpu.make_async_remote_copy(
-            best.at[group // 4, z_to], table.at[cluster], back_send, back_recv,
-            device_id=device(group // 2, z_to, group % 2, y_to), device_id_type=MESH
-        )
-
-    @pl.when(is_owner)
-    def _():
-        cluster = 16 * y + 2 * z + x // 2
-        me = (y * NZ + z) * GROUP + lane_group
+    @pl.when(is_owner)
+    def _():
         places = [(z_to, y_to) for z_to in range(NZ) for y_to in range(NY)]
         for z_to, y_to in sorted(places, key=lambda p: p[0] + (1.5 if p[1] else 0.0)):
             for group in range(GROUP):
-                @pl.when(me != (y_to * NZ + z_to) * GROUP + group)
-                def _():
-                    back(cluster, group, z_to, y_to).start()
+                if z_to or group >= NK:
+                    @pl.when(me != (y_to * NZ + z_to) * GROUP + group)
+                    def _():
+                        back(cluster, group, z_to, y_to).start()
 
         table[cluster] = best[lane_group // 4, z]
         pltpu.make_async_remote_copy(
@@ -316,6 +344,7 @@
             vmem((8, 128), jnp.int32),
             vmem((512, 128), jnp.bfloat16),
             vmem((2, NZ, 1, 128), jnp.float32),
+            vmem((1, 1, 128), jnp.float32),
             vmem((256, 1, 128), jnp.float32),
             dma,
             dma((NZ,)),

time: 47.4 us -> 46.7 us (0.985); the launches traced: 47.3 us -> 45.9 us
  Pallas kernels: 46.7 us -> 45.3 us
    pallas_call x1, Pallas kernels: 46.7 us -> 45.3 us  [local(): pl.pallas_call(kernel, out_shape=jax.ShapeDtypeStruct((8, 128), jnp.float...]
where the time goes in v6:
time: 46.7 us; the launch traced here: 45.9 us
  Pallas kernels  45.3 us (97%)
  local copies, waits for them, and re-layouts  0.6 us (1%)
    pallas_call x1, Pallas kernels, local(): pl.pallas_call(kernel, out_shape=jax.ShapeDtypeStruct((8, 128), jnp.float...  45.3 us

profile of v6, /device:TPU:1, one launch (start us, length us, event | category | flops | bytes accessed | tf_op | source)
XLA Modules:
  0.0 45.9 jit_solution(5439057670460484823)
XLA Ops:
  0.0 45.3 %shard_map.28 = f32[8,128]{1,0:T(8,128)S(1)} custom-call(bf16[1024,1024]{1,0:T(8,128)(2,1)} %emb_hbm.1, s32[8,128]{1,0:T(8,128)} %bitcast.3), custom_call_target="tpu_custom_call" | custom-call | tf_op jit(solution)/shard_map/pallas_call | solution.py:328
  45.3 0.6 %copy.4 = f32[1024]{0:T(1024)} copy(f32[1024]{0:T(1024)S(1)} %bitcast.2) | data formatting | bytes 8192

commit v7 on v6

--- a/solution.py
+++ b/solution.py
@@ -261,9 +261,18 @@
     def _():
         places = [(z_to, y_to) for z_to in range(NZ) for y_to in range(NY)]
         for z_to, y_to in sorted(places, key=lambda p: p[0] + (1.5 if p[1] else 0.0)):
-            for group in range(GROUP):
-                if z_to or group >= NK:
-                    @pl.when(me != (y_to * NZ + z_to) * GROUP + group)
+            groups = range(0 if z_to else NK, GROUP)
+            here = (z == z_to) & (y == y_to)
+
+            @pl.when(jnp.logical_not(here))
+            def _():
+                for group in groups:
+                    back(cluster, group, z_to, y_to).start()
+
+            @pl.when(here)
+            def _():
+                for group in groups:
+                    @pl.when(lane_group != group)
                     def _():
                         back(cluster, group, z_to, y_to).start()
 

time: 46.7 us -> 46.7 us (level)
  no operation moved by 1% of the time
where the time goes in v7:
time: 46.7 us; the launch traced here: 45.9 us
  Pallas kernels  45.3 us (97%)
  local copies, waits for them, and re-layouts  0.6 us (1%)
    pallas_call x1, Pallas kernels, local(): pl.pallas_call(kernel, out_shape=jax.ShapeDtypeStruct((8, 128), jnp.float...  45.3 us

profile of v7, /device:TPU:1, one launch (start us, length us, event | category | flops | bytes accessed | tf_op | source)
XLA Modules:
  0.0 45.9 jit_solution(12796896702689872065)
XLA Ops:
  0.0 45.3 %shard_map.28 = f32[8,128]{1,0:T(8,128)S(1)} custom-call(bf16[1024,1024]{1,0:T(8,128)(2,1)} %emb_hbm.1, s32[8,128]{1,0:T(8,128)} %bitcast.3), custom_call_target="tpu_custom_call" | custom-call | tf_op jit(solution)/shard_map/pallas_call | solution.py:337
  45.3 0.6 %copy.4 = f32[1024]{0:T(1024)} copy(f32[1024]{0:T(1024)S(1)} %bitcast.2) | data formatting | bytes 8192
